TPU v7x, 32 devices: a whole 2x2x4 slice. The times are simulated.
32 devices in a mesh: groups: 2 (over x), dp: 2 (over core), tensor: 8 (over z, y).
Axes of the slice: x: 2, y: 2, z: 4, core: 2. Of those that a mesh axis runs over, the one named last changes fastest.
Arguments:
- activations: bfloat16 [28672, 32768], P('tensor', ('groups', 'dp')), parts along dimension 1, may hold values from -6 to 6
- out_grads: bfloat16 [8192, 32768], P('tensor', ('groups', 'dp')), parts along dimension 1, may hold values from -6 to 6
- proj_in: bfloat16 [28672, 64], P('tensor'), may hold values from -0.03125 to 0.03125
- proj_out: bfloat16 [8192, 64], P('tensor'), may hold values from -0.0625 to 0.0625
- owners: int32 [16], P('groups'), parts along dimension 0, may hold values from 0 to 1, as said below
- valid_len: int32 [16], P(('groups', 'dp')), parts along dimension 0, may hold values from 256 to 2048
Outputs:
- logs: float32 [4, 4, 64, 64], P(('groups', 'dp'), None, 'tensor'), parts along dimension 0
There are 2 independent parts, one for each index of `groups`. A program takes and returns all parts, laid end to end along the dimension named above; an argument that names none is the same for every part. Nothing has to cross between parts.
Inputs may be any that keep to these rules, and one draw needn't show every extreme that they name: `owners`: every shard number 0 to 2 - 1 is named by exactly 4 sequences.
All inputs are finite; a program needn't handle non-finite values.
Results may differ from a plain program's by a relative error of at most 0.0003.
Values sent between devices are 32-bit elements; how exact they have to be, the bound alone decides.
A program may use at most 192 MiB of HBM per device.

v0:
```python
import jax
import jax.numpy as jnp
from jax import lax
from jax.sharding import PartitionSpec as P

SEQ_LEN = 2048


def project(weights, data):
    return lax.dot_general(
        weights, data, (((0,), (0,)), ((), ())), preferred_element_type=jnp.float32
    )


def local(activations, out_grads, proj_in, proj_out, owners, valid_len):
    rank_size = proj_in.shape[1]
    tokens = activations.shape[1]
    examples = tokens // SEQ_LEN
    shards = lax.axis_size("tensor")
    row_block = rank_size // shards
    my_index = lax.axis_index("tensor")
    grad_part = project(proj_out, out_grads)
    act_part = project(proj_in, activations)
    act_full, grad_full = lax.psum((act_part, grad_part), "tensor")
    act_rows = lax.dynamic_slice_in_dim(act_full, my_index * row_block, row_block, 0)
    positions = jnp.arange(SEQ_LEN, dtype=jnp.int32)
    weights = (positions[None, :] < valid_len[:, None]).astype(jnp.float32)
    left_rows = act_rows.reshape(row_block, examples, SEQ_LEN)
    right_rows = grad_full.reshape(rank_size, examples, SEQ_LEN) * weights[None]
    local_logs = jnp.einsum("rel,qel->erq", left_rows, right_rows, precision=lax.Precision.HIGHEST)
    local_logs = local_logs / jnp.sqrt(valid_len.astype(jnp.float32))[:, None, None]
    n_shards = lax.axis_size("dp")
    dp_index = lax.axis_index("dp")
    slot_ids = jnp.arange(examples, dtype=jnp.int32)
    my_owners = lax.dynamic_slice_in_dim(owners, dp_index * examples, examples, 0)
    targets = jnp.arange(n_shards, dtype=jnp.int32)
    matches = (my_owners[None, :] == targets[:, None]).astype(jnp.int32)
    slot_rank = jnp.cumsum(matches, axis=1) - matches
    packing = (matches[:, None, :] * (slot_rank[:, None, :] == slot_ids[None, :, None])).astype(
        jnp.float32
    )
    outgoing = jnp.einsum("oke,erq->okrq", packing, local_logs, precision=lax.Precision.HIGHEST)
    received = lax.all_to_all(outgoing, "dp", split_axis=0, concat_axis=0, tiled=True)
    owned_by_me = (owners.reshape(n_shards, examples) == dp_index).astype(jnp.int32)
    counts = jnp.sum(owned_by_me, axis=1)
    offsets = jnp.cumsum(counts) - counts
    valid_slot = slot_ids[None, :] < counts[:, None]
    target_pos = offsets[:, None] + slot_ids[None, :]
    placing = (valid_slot[None] & (target_pos[None] == slot_ids[:, None, None])).astype(jnp.float32)
    mine = jnp.einsum("psk,skrq->prq", placing, received, precision=lax.Precision.HIGHEST)
    return mine[None]


def solution(mesh):
    return jax.shard_map(
        local,
        mesh=mesh,
        in_specs=(
            P("tensor", ("groups", "dp")),
            P("tensor", ("groups", "dp")),
            P("tensor", None),
            P("tensor", None),
            P("groups"),
            P(("groups", "dp")),
        ),
        out_specs=P(("groups", "dp"), None, "tensor", None),
        check_vma=False,
    )
```

profile of v0, /device:TPU:0, one launch (start us, length us, event | category | flops | bytes accessed | tf_op | source)
XLA Modules:
  0.0 218.1 jit_solution(4446230694946408237)
XLA Ops:
  6.5 0.0 copy-start
  6.5 0.0 all-reduce.3.cloned.1.call-start
  6.5 8.9 %fusion.31 = f32[64,8192]{1,0:T(8,128)S(1)} fusion(bf16[1024,64]{0,1:T(8,128)(2,1)} %param.9, bf16[1024,8192]{1,0:T(8,128)(2,1)} %param.7), kind=kOutput, calls=%fused_computation.34 | convolution fusion | flops 1073741824 | bytes 19005440 | tf_op jit(solution)/shard_map/dot_general | solution.py:10
  15.5 2.4 %reshape.147 = f32[64,4,2048]{2,1,0:T(4,128)} reshape(f32[64,8192]{1,0:T(8,128)S(1)} %fusion.31) | data formatting | bytes 4194304 | tf_op jit(solution)/shard_map/reshape | solution.py:29
  17.9 0.0 copy-done
  17.9 22.1 %fusion.30 = f32[64,8192]{1,0:T(8,128)} fusion(bf16[3584,64]{0,1:T(8,128)(2,1)S(1)} %copy-done, bf16[3584,8192]{1,0:T(8,128)(2,1)} %param.6), kind=kOutput, calls=%fused_computation.33 | convolution fusion | flops 3758096384 | bytes 61276160 | tf_op jit(solution)/shard_map/dot_general | solution.py:10
  40.0 0.0 copy-start.3
  40.0 0.0 copy-start.2
  40.0 0.0 all-reduce.3.cloned.1.call-update
  40.0 0.6 copy-done.3
  40.6 0.1 reshape.148
  40.7 0.1 reduce_sum.9
  40.8 0.2 reduce-window.8
  41.0 0.1 dynamic_slice.6
  41.1 0.2 reduce_window_sum.18
  41.3 0.1 iota_compare_fusion.4
  41.3 0.0 copy-done.2
  41.4 0.1 iota_add_fusion
  41.4 0.1 fusion.8
  41.5 158.0 %all-reduce.3.cloned.1.call-done = (f32[64,8192]{1,0:T(8,128)}, f32[64,4,2048]{2,1,0:T(4,128)}) async-done(((f32[64,8192]{1,0:T(8,128)}, f32[64,4,2048]{2,1,0:T(4,128)}), (f32[64,8192]{1,0:T(8,128)}, f32[64,4,2048]{2,1,0:T(4,128)})) %all-reduce.3.cloned.1.call-update) | async-done | bytes 4194320 | tf_op jit(solution)/shard_map/psum | solution.py:24
  199.5 1.0 constant_dynamic-slice_fusion
  200.5 0.0 copy-start.1
  200.5 1.8 broadcast_multiply_fusion
  202.3 2.8 %fusion.5 = f32[4,8,64,1]{2,1,0,3:T(8,128)S(1)} fusion(f32[8,4,2048]{2,0,1:T(8,128)S(1)} %bitcast.39, f32[64,4,2048]{2,1,0:T(4,128)S(1)} %bitcast.37, f32[4]{0:T(128)S(1)} %convert_sqrt_fusion), kind=kOutput, calls=%fused_computation.4 | convolution fusion | flops 50333696 | bytes 2367504 | tf_op jit(solution)/shard_map/rel,qel->erq/dot_general | solution.py:30
  205.1 0.2 fusion.24
  205.3 0.1 reshape.153
  205.4 3.7 %all_to_all.5 = f32[2,1,2048]{2,1,0:T(1,128)S(1)} all-to-all(f32[2,1,2048]{2,1,0:T(1,128)S(1)} %reshape.153), channel_id=1, replica_groups=mesh['groups'=2,'dp'=2,'tensor'=8] {'dp'}, dimensions={0} | all-to-all | bytes 32768 | tf_op jit(solution)/shard_map/all_to_all | solution.py:43
  209.1 0.5 broadcast.69
  209.6 0.7 reduce
  210.3 0.1 reshape.154
  210.4 0.2 convolution_bitcast_fusion
  210.7 0.6 copy.9
  211.3 0.0 copy-done.1
  (6 shorter events, 0.0 us)
Async XLA Ops:
  6.5 11.4 %copy-start = (bf16[3584,64]{0,1:T(8,128)(2,1)S(1)}, bf16[3584,64]{0,1:T(8,128)(2,1)}, u32[]{:S(2)}) copy-start(bf16[3584,64]{0,1:T(8,128)(2,1)} %param.8) | copy-start | bytes 1376260
  6.5 192.9 %all-reduce.3.cloned.1.call-start = ((), (), s32[]{:S(2)}) async-start(), calls=%async_computation.1 | async-start | bytes 8388608 | tf_op jit(solution)/shard_map/psum | solution.py:24
  40.0 0.7 copy-start.3
  40.0 1.4 copy-start.2
  200.5 10.8 %copy-start.1 = (bf16[3584,64]{0,1:T(8,128)(2,1)S(1)}, bf16[3584,64]{0,1:T(8,128)(2,1)}, u32[]{:S(2)}) copy-start(bf16[3584,64]{0,1:T(8,128)(2,1)} %param.8) | copy-start | bytes 1376260
Sparse Core Ops, SparseCore 0:
  40.1 159.3 all-reduce.2
where the time goes:
time: 218 us
  waiting for transfers between devices  158 us (72%)
  matrix products  34.2 us (16%)
  between operations  13.5 us (6%)
  local copies, waits for them, and re-layouts  5.51 us (3%)
  blocking collectives  3.72 us (2%)
  other arithmetic  3.21 us (1%)
    psum x1, waiting for transfers between devices, local(): act_full, grad_full = lax.psum((act_part, grad_part), 'tensor')  158 us
    dot_general x2, matrix products, project(): lax.dot_general(weights, data, (((0,), (0,)), ((), ())), preferred_elemen...  31 us
  transfers between devices with their start and end apart: 1, of which 1 were waited for; matrix products, arithmetic and copies ran while one was open for 0% of the time, Pallas kernels for 0%

commit v1 on v0

--- a/solution.py
+++ b/solution.py
@@ -1,15 +1,290 @@
 import jax
 import jax.numpy as jnp
 from jax import lax
+from jax.experimental import pallas as pl
+from jax.experimental.pallas import tpu as pltpu
 from jax.sharding import PartitionSpec as P
 
 SEQ_LEN = 2048
+MESH = pl.DeviceIdType.MESH
+BLOCK = 512
+SLOTS = 3
+LAG_PAIR = 2
+LAG_HOP = 1
+LINE = 4
+PAIR = 2
 
 
 def project(weights, data):
     return lax.dot_general(
         weights, data, (((0,), (0,)), ((), ())), preferred_element_type=jnp.float32
     )
+
+
+def fused(
+    acts, grads, proj_in, proj_out, owners, valid_len, out,
+    abuf, gbuf, win, wout, part, got_pair, got_up, got_down, prods, rows, got_rows,
+    asem, gsem, pair_s, pair_r, up_s, up_r, down_s, down_r, row_s, row_r,
+):
+    dp = lax.axis_index("dp")
+    me = lax.axis_index("tensor")
+    z, y = me // PAIR, me % PAIR
+    tensor = LINE * PAIR
+    rank = proj_in.shape[1]
+    blocks = acts.shape[1] // BLOCK
+    per_seq = SEQ_LEN // BLOCK
+    half = BLOCK // PAIR
+    last = LINE - 1
+    n_all = 2 * tensor
+    lin = dp * tensor + me
+
+    def fetch(b):
+        slot = lax.rem(b, SLOTS)
+        cols = pl.ds(pl.multiple_of(b * BLOCK, BLOCK), BLOCK)
+        return (
+            pltpu.make_async_copy(acts.at[:, cols], abuf.at[slot], asem.at[slot]),
+            pltpu.make_async_copy(grads.at[:, cols], gbuf.at[slot], gsem.at[slot]),
+        )
+
+    for b in range(SLOTS):
+        for copy in fetch(jnp.int32(b)):
+            copy.start()
+
+    barrier = pltpu.get_barrier_semaphore()
+    for k in range(1, n_all):
+        other = lax.rem(lin + k, n_all)
+        pl.semaphore_signal(
+            barrier, inc=1, device_id={"dp": other // tensor, "tensor": other % tensor},
+            device_id_type=MESH,
+        )
+    win[...] = proj_in[...].astype(jnp.float32).T.astype(jnp.bfloat16)
+    wout[...] = proj_out[...].astype(jnp.float32).T.astype(jnp.bfloat16)
+    prods[...] = jnp.zeros_like(prods)
+    pl.semaphore_wait(barrier, n_all - 1)
+
+    def owner(j):
+        return (3 * j) % LINE
+
+    def pair_copy(j):
+        return pltpu.make_async_remote_copy(
+            src_ref=part.at[j, 1 - y], dst_ref=got_pair.at[j],
+            send_sem=pair_s.at[j], recv_sem=pair_r.at[j],
+            device_id={"tensor": z * PAIR + 1 - y}, device_id_type=MESH,
+        )
+
+    def up_copy(j, src):
+        return pltpu.make_async_remote_copy(
+            src_ref=src, dst_ref=got_up.at[j],
+            send_sem=up_s.at[j], recv_sem=up_r.at[j],
+            device_id={"tensor": (z + 1) * PAIR + y}, device_id_type=MESH,
+        )
+
+    def down_copy(j, src):
+        return pltpu.make_async_remote_copy(
+            src_ref=src, dst_ref=got_down.at[j],
+            send_sem=down_s.at[j], recv_sem=down_r.at[j],
+            device_id={"tensor": (z - 1) * PAIR + y}, device_id_type=MESH,
+        )
+
+    def step(b, carry):
+        @pl.when(b < blocks)
+        def _():
+            slot = lax.rem(b, SLOTS)
+            for copy in fetch(b):
+                copy.wait()
+            left = jnp.dot(win[...], abuf[slot], preferred_element_type=jnp.float32)
+            right = jnp.dot(wout[...], gbuf[slot], preferred_element_type=jnp.float32)
+            for h in range(PAIR):
+                part[b, h, :rank, :] = left[:, h * half:(h + 1) * half]
+                part[b, h, rank:, :] = right[:, h * half:(h + 1) * half]
+            pair_copy(b).start()
+
+            @pl.when(b + SLOTS < blocks)
+            def _():
+                for copy in fetch(b + SLOTS):
+                    copy.start()
+
+        j0 = b - LAG_PAIR
+
+        @pl.when((j0 >= 0) & (j0 < blocks))
+        def _():
+            pair_copy(j0).wait()
+            part[j0, y] = part[j0, y] + got_pair[j0]
+
+            @pl.when((z == 0) & (owner(j0) > 0))
+            def _():
+                up_copy(j0, part.at[j0, y]).start()
+
+            @pl.when((z == last) & (owner(j0) < last))
+            def _():
+                down_copy(j0, part.at[j0, y]).start()
+
+        for dist in range(1, last):
+            j = b - LAG_PAIR - dist * LAG_HOP
+            inside = (j >= 0) & (j < blocks)
+
+            @pl.when(inside & (z == dist) & (owner(j) > z))
+            def _():
+                copy = up_copy(j, got_up.at[j])
+                copy.wait_recv()
+                got_up[j] = got_up[j] + part[j, y]
+                copy.start()
+
+            @pl.when(inside & (z == last - dist) & (owner(j) < z))
+            def _():
+                copy = down_copy(j, got_down.at[j])
+                copy.wait_recv()
+                got_down[j] = got_down[j] + part[j, y]
+                copy.start()
+
+        j3 = b - LAG_PAIR - LAG_HOP * jnp.maximum(z, last - z)
+
+        @pl.when((j3 >= 0) & (j3 < blocks) & (owner(j3) == z))
+        def _():
+            @pl.when(z > 0)
+            def _():
+                up_copy(j3, got_up.at[j3]).wait_recv()
+                part[j3, y] = part[j3, y] + got_up[j3]
+
+            @pl.when(z < last)
+            def _():
+                down_copy(j3, got_down.at[j3]).wait_recv()
+                part[j3, y] = part[j3, y] + got_down[j3]
+
+            seq = j3 // per_seq
+            total = part[j3, y]
+            first = (j3 % per_seq) * BLOCK + y * half
+            place = first + lax.broadcasted_iota(jnp.int32, (rank, half), 1)
+            a = total[:rank]
+            g = jnp.where(place < valid_len[seq], total[rank:], 0.0)
+            a_hi = a.astype(jnp.bfloat16)
+            g_hi = g.astype(jnp.bfloat16)
+            a_lo = (a - a_hi.astype(jnp.float32)).astype(jnp.bfloat16)
+            g_lo = (g - g_hi.astype(jnp.float32)).astype(jnp.bfloat16)
+            prods[seq] = prods[seq] + lax.dot_general(
+                jnp.concatenate([a_hi, a_lo], 0), jnp.concatenate([g_hi, g_lo], 0),
+                (((1,), (1,)), ((), ())), preferred_element_type=jnp.float32,
+            )
+
+        return carry
+
+    lax.fori_loop(0, blocks + LAG_PAIR + LAG_HOP * last, step, 0)
+
+    seqs = blocks // per_seq
+    block_rows = rank // tensor
+    for p in range(seqs // 2):
+        halves = []
+        for e in (2 * p, 2 * p + 1):
+            q = prods[e]
+            full = (
+                q[rank:, rank:] + q[:rank, rank:] + q[rank:, :rank] + q[:rank, :rank]
+            )
+            length = jnp.full((rank, rank), valid_len[e], jnp.int32).astype(jnp.float32)
+            halves.append(full / jnp.sqrt(length))
+        both = jnp.concatenate(halves, 1)
+        for r in range(tensor):
+            rows[r, p] = both[r * block_rows:(r + 1) * block_rows]
+
+    def row_copy(k):
+        to = lax.rem(lin + k, n_all)
+        return pltpu.make_async_remote_copy(
+            src_ref=rows.at[to % tensor], dst_ref=got_rows.at[lin],
+            send_sem=row_s.at[k], recv_sem=row_r.at[lin],
+            device_id={"dp": to // tensor, "tensor": to % tensor}, device_id_type=MESH,
+        )
+
+    def row_arrival(k):
+        source = lax.rem(lin + n_all - k, n_all)
+        return pltpu.make_async_remote_copy(
+            src_ref=rows.at[0], dst_ref=got_rows.at[source],
+            send_sem=row_s.at[k], recv_sem=row_r.at[source],
+            device_id={"dp": source // tensor, "tensor": source % tensor}, device_id_type=MESH,
+        )
+
+    for k in range(1, n_all):
+        row_copy(k).start()
+    got_rows[lin] = rows[me]
+
+    def drain(j, carry):
+        @pl.when((z < last) & (owner(j) > z))
+        def _():
+            up_copy(j, part.at[j, y]).wait_send()
+
+        @pl.when((z > 0) & (owner(j) < z))
+        def _():
+            down_copy(j, part.at[j, y]).wait_send()
+
+        return carry
+
+    lax.fori_loop(0, blocks, drain, 0)
+    for k in range(1, n_all):
+        row_arrival(k).wait_recv()
+
+    held = []
+    for shard in range(2):
+        total = got_rows[shard * tensor]
+        for r in range(1, tensor):
+            total = total + got_rows[shard * tensor + r]
+        for e in range(seqs):
+            held.append(total[e // 2][:, (e % 2) * rank:(e % 2 + 1) * rank])
+    count = jnp.int32(0)
+    places = [jnp.zeros_like(held[0])] * seqs
+    for e, record in enumerate(held):
+        mine = owners[e] == dp
+        for s in range(seqs):
+            share = jnp.where(mine & (count == s), 1.0, 0.0)
+            places[s] = places[s] + share * record
+        count = count + mine.astype(jnp.int32)
+    for s in range(seqs):
+        out[s] = places[s]
+    for k in range(1, n_all):
+        row_copy(k).wait_send()
+
+
+def fused_local(acts, grads, proj_in, proj_out, owners, valid_len):
+    rank = proj_in.shape[1]
+    tokens = acts.shape[1]
+    blocks = tokens // BLOCK
+    half = BLOCK // PAIR
+    seqs = tokens // SEQ_LEN
+    tensor = LINE * PAIR
+    block_rows = rank // tensor
+    vmem = pl.BlockSpec(memory_space=pltpu.VMEM)
+    smem = pl.BlockSpec(memory_space=pltpu.SMEM)
+    anywhere = pl.BlockSpec(memory_space=pl.ANY)
+    sems = pltpu.SemaphoreType.DMA
+    stage = pltpu.VMEM((blocks, 2 * rank, half), jnp.float32)
+    flops = 2 * rank * tokens * (acts.shape[0] + grads.shape[0])
+    logs = pl.pallas_call(
+        fused,
+        out_shape=jax.ShapeDtypeStruct((seqs, block_rows, rank), jnp.float32),
+        in_specs=[anywhere, anywhere, vmem, vmem, smem, smem],
+        out_specs=vmem,
+        scratch_shapes=[
+            pltpu.VMEM((SLOTS, acts.shape[0], BLOCK), acts.dtype),
+            pltpu.VMEM((SLOTS, grads.shape[0], BLOCK), grads.dtype),
+            pltpu.VMEM((rank, acts.shape[0]), acts.dtype),
+            pltpu.VMEM((rank, grads.shape[0]), grads.dtype),
+            pltpu.VMEM((blocks, PAIR, 2 * rank, half), jnp.float32),
+            stage, stage, stage,
+            pltpu.VMEM((seqs, 2 * rank, 2 * rank), jnp.float32),
+            pltpu.VMEM((tensor, seqs // 2, block_rows, 2 * rank), jnp.float32),
+            pltpu.VMEM((2 * tensor, seqs // 2, block_rows, 2 * rank), jnp.float32),
+            sems((SLOTS,)), sems((SLOTS,)),
+            sems((blocks,)), sems((blocks,)),
+            sems((blocks,)), sems((blocks,)),
+            sems((blocks,)), sems((blocks,)),
+            sems((2 * tensor,)), sems((2 * tensor,)),
+        ],
+        compiler_params=pltpu.CompilerParams(
+            collective_id=0, has_side_effects=True, vmem_limit_bytes=48 * 2**20
+        ),
+        cost_estimate=pl.CostEstimate(
+            flops=flops, bytes_accessed=2 * tokens * (acts.shape[0] + grads.shape[0]),
+            transcendentals=0,
+        ),
+    )(acts, grads, proj_in, proj_out, owners, valid_len)
+    return logs[None]
 
 
 def local(activations, out_grads, proj_in, proj_out, owners, valid_len):
@@ -52,8 +327,9 @@
 
 
 def solution(mesh):
+    fits = mesh.shape["tensor"] == LINE * PAIR and mesh.shape["dp"] == 2
     return jax.shard_map(
-        local,
+        fused_local if fits else local,
         mesh=mesh,
         in_specs=(
             P("tensor", ("groups", "dp")),

time: 218 us -> 76.4 us (0.35)
  waiting for transfers between devices: 158 us -> 0 us
  Pallas kernels: 0 us -> 71.7 us
  matrix products: 34.2 us -> 0 us
  between operations: 13.5 us -> 0.03 us
  blocking collectives: 3.72 us -> 0 us
  other arithmetic: 3.21 us -> 0 us
    psum x1 -> x0, waiting for transfers between devices: 158 us -> none  [local(): act_full, grad_full = lax.psum((act_part, grad_part), 'tensor')]
    pallas_call x0 -> x1, Pallas kernels: none -> 71.7 us  [fused_local(): pl.pallas_call(fused, out_shape=jax.ShapeDtypeStruct((seqs, block_rows, r...]
    dot_general x5 -> x0, matrix products: 34.2 us -> none  [the longest x2 31 us: project(): lax.dot_general(weights, data, (((0,), (0,)), ((), ())), preferred_elemen...]
    all_to_all x1 -> x0, blocking collectives: 3.72 us -> none  [local(): lax.all_to_all(outgoing, 'dp', split_axis=0, concat_axis=0, tiled=True)]
    unnamed x11 -> x7, local copies, waits for them, and re-layouts: 0.84 us -> 4.43 us
    reshape x1 -> x0, local copies, waits for them, and re-layouts: 2.43 us -> none  [local(): right_rows = grad_full.reshape(rank_size, examples, SEQ_LEN) * weights[None]]
  transfers between devices with their start and end apart: 1 -> 0, of which waited for: 1 -> 0; matrix products, arithmetic and copies ran while one was open for 0% -> 0% of each run, Pallas kernels for 0% -> 0%
where the time goes in v1:
time: 76.4 us; the launch traced here: 76.2 us
  Pallas kernels  71.7 us (94%)
  local copies, waits for them, and re-layouts  4.43 us (6%)
    pallas_call x1, Pallas kernels, fused_local(): pl.pallas_call(fused, out_shape=jax.ShapeDtypeStruct((seqs, block_rows, r...  71.7 us
    unnamed x7, local copies, waits for them, and re-layouts  4.43 us

profile of v1, /device:TPU:0, one launch (start us, length us, event | category | flops | bytes accessed | tf_op | source)
XLA Modules:
  0.0 76.2 jit_solution(8281473858237452196)
XLA Ops:
  0.0 1.1 %copy.8.proj_out = bf16[1024,64]{1,0:T(8,128)(2,1)S(1)} copy(bf16[1024,64]{0,1:T(8,128)(2,1)} %param.9) | data formatting | bytes 262144 | tf_op args[3]
  1.1 1.4 %copy.7.proj_in = bf16[3584,64]{1,0:T(8,128)(2,1)S(1)} copy(bf16[3584,64]{0,1:T(8,128)(2,1)} %param.8) | data formatting | bytes 917504 | tf_op args[2]
  2.5 0.0 copy-start
  2.5 0.6 copy-done
  3.2 0.0 copy-start.1
  3.2 0.7 copy-done.1
  3.8 71.7 %shard_map.64 = f32[4,8,64]{2,1,0:T(8,128)S(1)} custom-call(bf16[3584,8192]{1,0:T(8,128)(2,1)} %acts.1, bf16[1024,8192]{1,0:T(8,128)(2,1)} %grads.1, bf16[3584,64]{1,0:T(8,128)(2,1)S(1)} %copy.7.proj_in, bf16[1024,64]{1,0:T(8,128)(2,1)S(1)} %copy.8.proj_out, s32[8]{0:T(128)S(1)} %copy-done, s32[4]{0:T(128)S(1)} %copy-done.1), custom_call_target="tpu_custom_call" | custom-call | flops 4831838208 | bytes 75497472 | tf_op jit(solution)/shard_map/pallas_call | solution.py:258
  75.6 0.6 copy.10
Async XLA Ops:
  2.5 0.7 copy-start
  3.2 0.7 copy-start.1

commit v2 on v1

--- a/solution.py
+++ b/solution.py
@@ -9,8 +9,11 @@
 MESH = pl.DeviceIdType.MESH
 BLOCK = 512
 SLOTS = 3
-LAG_PAIR = 2
-LAG_HOP = 1
+QUARTERS = 4
+LAG_PAIR = 4
+LAG_HOP = 3
+LAG_TWO = 3
+LAG_LAST = 3
 LINE = 4
 PAIR = 2
 
@@ -22,18 +25,18 @@
 
 
 def fused(
-    acts, grads, proj_in, proj_out, owners, valid_len, out,
-    abuf, gbuf, win, wout, part, got_pair, got_up, got_down, prods, rows, got_rows,
-    asem, gsem, pair_s, pair_r, up_s, up_r, down_s, down_r, row_s, row_r,
+    acts, grads, win, wout, owners, valid_len, out,
+    abuf, gbuf, part, got_pair, got_one, got_two, got_last, prods, rows, got_rows,
+    asem, gsem, pair_s, pair_r, one_s, one_r, two_s, two_r, last_s, last_r, row_s, row_r,
 ):
     dp = lax.axis_index("dp")
     me = lax.axis_index("tensor")
     z, y = me // PAIR, me % PAIR
     tensor = LINE * PAIR
-    rank = proj_in.shape[1]
+    rank = win.shape[0]
     blocks = acts.shape[1] // BLOCK
     per_seq = SEQ_LEN // BLOCK
-    half = BLOCK // PAIR
+    width = BLOCK // QUARTERS
     last = LINE - 1
     n_all = 2 * tensor
     lin = dp * tensor + me
@@ -57,33 +60,67 @@
             barrier, inc=1, device_id={"dp": other // tensor, "tensor": other % tensor},
             device_id_type=MESH,
         )
-    win[...] = proj_in[...].astype(jnp.float32).T.astype(jnp.bfloat16)
-    wout[...] = proj_out[...].astype(jnp.float32).T.astype(jnp.bfloat16)
     prods[...] = jnp.zeros_like(prods)
     pl.semaphore_wait(barrier, n_all - 1)
 
-    def owner(j):
-        return (3 * j) % LINE
+    peer = z * PAIR + 1 - y
+
+    def way_one(j):
+        return 2 * (j % 2) - 1
+
+    def way_two(j):
+        return 1 - 2 * (j % 2)
+
+    def begin(way):
+        return last * (1 - way) // 2
+
+    def end(way):
+        return last * (1 + way) // 2
 
     def pair_copy(j):
         return pltpu.make_async_remote_copy(
             src_ref=part.at[j, 1 - y], dst_ref=got_pair.at[j],
             send_sem=pair_s.at[j], recv_sem=pair_r.at[j],
-            device_id={"tensor": z * PAIR + 1 - y}, device_id_type=MESH,
-        )
-
-    def up_copy(j, src):
-        return pltpu.make_async_remote_copy(
-            src_ref=src, dst_ref=got_up.at[j],
-            send_sem=up_s.at[j], recv_sem=up_r.at[j],
-            device_id={"tensor": (z + 1) * PAIR + y}, device_id_type=MESH,
-        )
-
-    def down_copy(j, src):
-        return pltpu.make_async_remote_copy(
-            src_ref=src, dst_ref=got_down.at[j],
-            send_sem=down_s.at[j], recv_sem=down_r.at[j],
-            device_id={"tensor": (z - 1) * PAIR + y}, device_id_type=MESH,
+            device_id={"tensor": peer}, device_id_type=MESH,
+        )
+
+    def last_copy(j):
+        return pltpu.make_async_remote_copy(
+            src_ref=part.at[j, PAIR + 1 - y], dst_ref=got_last.at[j],
+            send_sem=last_s.at[j], recv_sem=last_r.at[j],
+            device_id={"tensor": peer}, device_id_type=MESH,
+        )
+
+    def one_copy(j, src):
+        return pltpu.make_async_remote_copy(
+            src_ref=src, dst_ref=got_one.at[j],
+            send_sem=one_s.at[j], recv_sem=one_r.at[j],
+            device_id={"tensor": (z + way_one(j)) * PAIR + y}, device_id_type=MESH,
+        )
+
+    def two_copy(j, src):
+        return pltpu.make_async_remote_copy(
+            src_ref=src, dst_ref=got_two.at[j],
+            send_sem=two_s.at[j], recv_sem=two_r.at[j],
+            device_id={"tensor": (z + way_two(j)) * PAIR + y}, device_id_type=MESH,
+        )
+
+    def both(j):
+        return part.at[j, pl.ds(PAIR, PAIR)]
+
+    def multiply(j, total, offset):
+        seq = j // per_seq
+        first = (j % per_seq) * BLOCK + offset
+        place = first + lax.broadcasted_iota(jnp.int32, (rank, width), 1)
+        a = total[:rank]
+        g = jnp.where(place < valid_len[seq], total[rank:], 0.0)
+        a_hi = a.astype(jnp.bfloat16)
+        g_hi = g.astype(jnp.bfloat16)
+        a_lo = (a - a_hi.astype(jnp.float32)).astype(jnp.bfloat16)
+        g_lo = (g - g_hi.astype(jnp.float32)).astype(jnp.bfloat16)
+        prods[seq] = prods[seq] + lax.dot_general(
+            jnp.concatenate([a_hi, a_lo], 0), jnp.concatenate([g_hi, g_lo], 0),
+            (((1,), (1,)), ((), ())), preferred_element_type=jnp.float32,
         )
 
     def step(b, carry):
@@ -94,10 +131,14 @@
                 copy.wait()
             left = jnp.dot(win[...], abuf[slot], preferred_element_type=jnp.float32)
             right = jnp.dot(wout[...], gbuf[slot], preferred_element_type=jnp.float32)
-            for h in range(PAIR):
-                part[b, h, :rank, :] = left[:, h * half:(h + 1) * half]
-                part[b, h, rank:, :] = right[:, h * half:(h + 1) * half]
+            for h in range(QUARTERS):
+                part[b, h, :rank, :] = left[:, h * width:(h + 1) * width]
+                part[b, h, rank:, :] = right[:, h * width:(h + 1) * width]
             pair_copy(b).start()
+
+            @pl.when(z == begin(way_two(b)))
+            def _():
+                two_copy(b, both(b)).start()
 
             @pl.when(b + SLOTS < blocks)
             def _():
@@ -111,64 +152,55 @@
             pair_copy(j0).wait()
             part[j0, y] = part[j0, y] + got_pair[j0]
 
-            @pl.when((z == 0) & (owner(j0) > 0))
-            def _():
-                up_copy(j0, part.at[j0, y]).start()
-
-            @pl.when((z == last) & (owner(j0) < last))
-            def _():
-                down_copy(j0, part.at[j0, y]).start()
+            @pl.when(z == begin(way_one(j0)))
+            def _():
+                one_copy(j0, part.at[j0, y]).start()
 
         for dist in range(1, last):
-            j = b - LAG_PAIR - dist * LAG_HOP
-            inside = (j >= 0) & (j < blocks)
-
-            @pl.when(inside & (z == dist) & (owner(j) > z))
-            def _():
-                copy = up_copy(j, got_up.at[j])
+            j1 = b - LAG_PAIR - dist * LAG_HOP
+
+            @pl.when((j1 >= 0) & (j1 < blocks) & (z == begin(way_one(j1)) + dist * way_one(j1)))
+            def _():
+                copy = one_copy(j1, got_one.at[j1])
                 copy.wait_recv()
-                got_up[j] = got_up[j] + part[j, y]
+                got_one[j1] = got_one[j1] + part[j1, y]
                 copy.start()
 
-            @pl.when(inside & (z == last - dist) & (owner(j) < z))
-            def _():
-                copy = down_copy(j, got_down.at[j])
+            j2 = b - dist * LAG_TWO
+
+            @pl.when((j2 >= 0) & (j2 < blocks) & (z == begin(way_two(j2)) + dist * way_two(j2)))
+            def _():
+                copy = two_copy(j2, got_two.at[j2])
                 copy.wait_recv()
-                got_down[j] = got_down[j] + part[j, y]
+                got_two[j2] = got_two[j2] + part[j2, PAIR:]
                 copy.start()
 
-        j3 = b - LAG_PAIR - LAG_HOP * jnp.maximum(z, last - z)
-
-        @pl.when((j3 >= 0) & (j3 < blocks) & (owner(j3) == z))
-        def _():
-            @pl.when(z > 0)
-            def _():
-                up_copy(j3, got_up.at[j3]).wait_recv()
-                part[j3, y] = part[j3, y] + got_up[j3]
-
-            @pl.when(z < last)
-            def _():
-                down_copy(j3, got_down.at[j3]).wait_recv()
-                part[j3, y] = part[j3, y] + got_down[j3]
-
-            seq = j3 // per_seq
-            total = part[j3, y]
-            first = (j3 % per_seq) * BLOCK + y * half
-            place = first + lax.broadcasted_iota(jnp.int32, (rank, half), 1)
-            a = total[:rank]
-            g = jnp.where(place < valid_len[seq], total[rank:], 0.0)
-            a_hi = a.astype(jnp.bfloat16)
-            g_hi = g.astype(jnp.bfloat16)
-            a_lo = (a - a_hi.astype(jnp.float32)).astype(jnp.bfloat16)
-            g_lo = (g - g_hi.astype(jnp.float32)).astype(jnp.bfloat16)
-            prods[seq] = prods[seq] + lax.dot_general(
-                jnp.concatenate([a_hi, a_lo], 0), jnp.concatenate([g_hi, g_lo], 0),
-                (((1,), (1,)), ((), ())), preferred_element_type=jnp.float32,
-            )
+        j3 = b - last * LAG_TWO
+
+        @pl.when((j3 >= 0) & (j3 < blocks) & (z == end(way_two(j3))))
+        def _():
+            two_copy(j3, got_two.at[j3]).wait_recv()
+            part[j3, PAIR:] = part[j3, PAIR:] + got_two[j3]
+            last_copy(j3).start()
+
+        j4 = b - LAG_PAIR - last * LAG_HOP
+
+        @pl.when((j4 >= 0) & (j4 < blocks) & (z == end(way_one(j4))))
+        def _():
+            one_copy(j4, got_one.at[j4]).wait_recv()
+            multiply(j4, part[j4, y] + got_one[j4], y * width)
+
+        j5 = b - last * LAG_TWO - LAG_LAST
+
+        @pl.when((j5 >= 0) & (j5 < blocks) & (z == end(way_two(j5))))
+        def _():
+            last_copy(j5).wait()
+            multiply(j5, part[j5, PAIR + y] + got_last[j5], (PAIR + y) * width)
 
         return carry
 
-    lax.fori_loop(0, blocks + LAG_PAIR + LAG_HOP * last, step, 0)
+    steps = blocks + max(LAG_PAIR + LAG_HOP * last, LAG_TWO * last + LAG_LAST)
+    lax.fori_loop(0, steps, step, 0)
 
     seqs = blocks // per_seq
     block_rows = rank // tensor
@@ -181,9 +213,9 @@
             )
             length = jnp.full((rank, rank), valid_len[e], jnp.int32).astype(jnp.float32)
             halves.append(full / jnp.sqrt(length))
-        both = jnp.concatenate(halves, 1)
+        record = jnp.concatenate(halves, 1)
         for r in range(tensor):
-            rows[r, p] = both[r * block_rows:(r + 1) * block_rows]
+            rows[r, p] = record[r * block_rows:(r + 1) * block_rows]
 
     def row_copy(k):
         to = lax.rem(lin + k, n_all)
@@ -206,13 +238,13 @@
     got_rows[lin] = rows[me]
 
     def drain(j, carry):
-        @pl.when((z < last) & (owner(j) > z))
-        def _():
-            up_copy(j, part.at[j, y]).wait_send()
-
-        @pl.when((z > 0) & (owner(j) < z))
-        def _():
-            down_copy(j, part.at[j, y]).wait_send()
+        @pl.when(z != end(way_one(j)))
+        def _():
+            one_copy(j, part.at[j, y]).wait_send()
+
+        @pl.when(z != end(way_two(j)))
+        def _():
+            two_copy(j, both(j)).wait_send()
 
         return carry
 
@@ -245,7 +277,7 @@
     rank = proj_in.shape[1]
     tokens = acts.shape[1]
     blocks = tokens // BLOCK
-    half = BLOCK // PAIR
+    width = BLOCK // QUARTERS
     seqs = tokens // SEQ_LEN
     tensor = LINE * PAIR
     block_rows = rank // tensor
@@ -253,7 +285,7 @@
     smem = pl.BlockSpec(memory_space=pltpu.SMEM)
     anywhere = pl.BlockSpec(memory_space=pl.ANY)
     sems = pltpu.SemaphoreType.DMA
-    stage = pltpu.VMEM((blocks, 2 * rank, half), jnp.float32)
+    stage = pltpu.VMEM((blocks, 2 * rank, width), jnp.float32)
     flops = 2 * rank * tokens * (acts.shape[0] + grads.shape[0])
     logs = pl.pallas_call(
         fused,
@@ -263,14 +295,15 @@
         scratch_shapes=[
             pltpu.VMEM((SLOTS, acts.shape[0], BLOCK), acts.dtype),
             pltpu.VMEM((SLOTS, grads.shape[0], BLOCK), grads.dtype),
-            pltpu.VMEM((rank, acts.shape[0]), acts.dtype),
-            pltpu.VMEM((rank, grads.shape[0]), grads.dtype),
-            pltpu.VMEM((blocks, PAIR, 2 * rank, half), jnp.float32),
-            stage, stage, stage,
+            pltpu.VMEM((blocks, QUARTERS, 2 * rank, width), jnp.float32),
+            stage, stage,
+            pltpu.VMEM((blocks, PAIR, 2 * rank, width), jnp.float32),
+            stage,
             pltpu.VMEM((seqs, 2 * rank, 2 * rank), jnp.float32),
             pltpu.VMEM((tensor, seqs // 2, block_rows, 2 * rank), jnp.float32),
             pltpu.VMEM((2 * tensor, seqs // 2, block_rows, 2 * rank), jnp.float32),
             sems((SLOTS,)), sems((SLOTS,)),
+            sems((blocks,)), sems((blocks,)),
             sems((blocks,)), sems((blocks,)),
             sems((blocks,)), sems((blocks,)),
             sems((blocks,)), sems((blocks,)),
@@ -283,7 +316,7 @@
             flops=flops, bytes_accessed=2 * tokens * (acts.shape[0] + grads.shape[0]),
             transcendentals=0,
         ),
-    )(acts, grads, proj_in, proj_out, owners, valid_len)
+    )(acts, grads, proj_in.T, proj_out.T, owners, valid_len)
     return logs[None]
 
 

time: 76.4 us -> 66.6 us (0.87)
  Pallas kernels: 71.7 us -> 62.6 us
    pallas_call x1, Pallas kernels: 71.7 us -> 62.6 us  [fused_local(): pl.pallas_call(fused, out_shape=jax.ShapeDtypeStruct((seqs, block_rows, r...]
    unnamed x7 -> x9, local copies, waits for them, and re-layouts: 4.43 us -> 3.84 us
where the time goes in v2:
time: 66.6 us; the launch traced here: 66.4 us
  Pallas kernels  62.6 us (94%)
  local copies, waits for them, and re-layouts  3.84 us (6%)
    pallas_call x1, Pallas kernels, fused_local(): pl.pallas_call(fused, out_shape=jax.ShapeDtypeStruct((seqs, block_rows, r...  62.6 us
    unnamed x9, local copies, waits for them, and re-layouts  3.84 us

profile of v2, /device:TPU:0, one launch (start us, length us, event | category | flops | bytes accessed | tf_op | source)
XLA Modules:
  0.0 66.4 jit_solution(9421174464292642601)
XLA Ops:
  0.0 0.0 copy-start
  0.0 1.0 %copy-done = bf16[3584,64]{0,1:T(8,128)(2,1)S(1)} copy-done((bf16[3584,64]{0,1:T(8,128)(2,1)S(1)}, bf16[3584,64]{0,1:T(8,128)(2,1)}, u32[]{:S(2)}) %copy-start) | copy-done | bytes 458776
  1.0 0.0 copy-start.1
  1.0 0.9 %copy-done.1 = bf16[1024,64]{0,1:T(8,128)(2,1)S(1)} copy-done((bf16[1024,64]{0,1:T(8,128)(2,1)S(1)}, bf16[1024,64]{0,1:T(8,128)(2,1)}, u32[]{:S(2)}) %copy-start.1) | copy-done | bytes 131096
  1.9 0.0 copy-start.2
  1.9 0.7 copy-done.2
  2.6 0.0 copy-start.3
  2.6 0.7 copy-done.3
  3.2 62.6 %shard_map.64 = f32[4,8,64]{2,1,0:T(8,128)S(1)} custom-call(bf16[3584,8192]{1,0:T(8,128)(2,1)} %acts.1, bf16[1024,8192]{1,0:T(8,128)(2,1)} %grads.1, bf16[64,3584]{1,0:T(8,128)(2,1)S(1)} %bitcast.3, bf16[64,1024]{1,0:T(8,128)(2,1)S(1)} %bitcast.4, s32[8]{0:T(128)S(1)} %copy-done.2, s32[4]{0:T(128)S(1)} %copy-done.3), custom_call_target="tpu_custom_call" | custom-call | flops 4831838208 | bytes 75497472 | tf_op jit(solution)/shard_map/pallas_call | solution.py:290
  65.8 0.6 copy.8
Async XLA Ops:
  0.0 1.0 %copy-start = (bf16[3584,64]{0,1:T(8,128)(2,1)S(1)}, bf16[3584,64]{0,1:T(8,128)(2,1)}, u32[]{:S(2)}) copy-start(bf16[3584,64]{0,1:T(8,128)(2,1)} %param.8) | copy-start | bytes 1376260
  1.0 0.9 %copy-start.1 = (bf16[1024,64]{0,1:T(8,128)(2,1)S(1)}, bf16[1024,64]{0,1:T(8,128)(2,1)}, u32[]{:S(2)}) copy-start(bf16[1024,64]{0,1:T(8,128)(2,1)} %param.9) | copy-start | bytes 393220
  1.9 0.7 copy-start.2
  2.6 0.7 copy-start.3

commit v3 on v2

--- a/solution.py
+++ b/solution.py
@@ -25,9 +25,9 @@
 
 
 def fused(
-    acts, grads, win, wout, owners, valid_len, out,
-    abuf, gbuf, part, got_pair, got_one, got_two, got_last, prods, rows, got_rows,
-    asem, gsem, pair_s, pair_r, one_s, one_r, two_s, two_r, last_s, last_r, row_s, row_r,
+    acts, grads, proj_in, proj_out, owners, valid_len, out,
+    abuf, gbuf, win, wout, part, got_pair, got_one, got_two, got_last, prods, rows, got_rows,
+    asem, gsem, pair_s, pair_r, one_s, one_r, two_s, two_r, last_s, last_r, row_s, row_r, wsem,
 ):
     dp = lax.axis_index("dp")
     me = lax.axis_index("tensor")
@@ -53,6 +53,12 @@
         for copy in fetch(jnp.int32(b)):
             copy.start()
 
+    weights = (
+        pltpu.make_async_copy(proj_in, win, wsem.at[0]),
+        pltpu.make_async_copy(proj_out, wout, wsem.at[1]),
+    )
+    for copy in weights:
+        copy.start()
     barrier = pltpu.get_barrier_semaphore()
     for k in range(1, n_all):
         other = lax.rem(lin + k, n_all)
@@ -62,6 +68,8 @@
         )
     prods[...] = jnp.zeros_like(prods)
     pl.semaphore_wait(barrier, n_all - 1)
+    for copy in weights:
+        copy.wait()
 
     peer = z * PAIR + 1 - y
 
@@ -284,17 +292,20 @@
     vmem = pl.BlockSpec(memory_space=pltpu.VMEM)
     smem = pl.BlockSpec(memory_space=pltpu.SMEM)
     anywhere = pl.BlockSpec(memory_space=pl.ANY)
+    hbm = pl.BlockSpec(memory_space=pltpu.HBM)
     sems = pltpu.SemaphoreType.DMA
     stage = pltpu.VMEM((blocks, 2 * rank, width), jnp.float32)
     flops = 2 * rank * tokens * (acts.shape[0] + grads.shape[0])
     logs = pl.pallas_call(
         fused,
         out_shape=jax.ShapeDtypeStruct((seqs, block_rows, rank), jnp.float32),
-        in_specs=[anywhere, anywhere, vmem, vmem, smem, smem],
+        in_specs=[anywhere, anywhere, hbm, hbm, smem, smem],
         out_specs=vmem,
         scratch_shapes=[
             pltpu.VMEM((SLOTS, acts.shape[0], BLOCK), acts.dtype),
             pltpu.VMEM((SLOTS, grads.shape[0], BLOCK), grads.dtype),
+            pltpu.VMEM((rank, acts.shape[0]), acts.dtype),
+            pltpu.VMEM((rank, grads.shape[0]), grads.dtype),
             pltpu.VMEM((blocks, QUARTERS, 2 * rank, width), jnp.float32),
             stage, stage,
             pltpu.VMEM((blocks, PAIR, 2 * rank, width), jnp.float32),
@@ -307,7 +318,7 @@
             sems((blocks,)), sems((blocks,)),
             sems((blocks,)), sems((blocks,)),
             sems((blocks,)), sems((blocks,)),
-            sems((2 * tensor,)), sems((2 * tensor,)),
+            sems((2 * tensor,)), sems((2 * tensor,)), sems((2,)),
         ],
         compiler_params=pltpu.CompilerParams(
             collective_id=0, has_side_effects=True, vmem_limit_bytes=48 * 2**20

time: 66.6 us -> 66.6 us (level)
  no operation moved by 1% of the time
where the time goes in v3:
time: 66.6 us; the launch traced here: 66.5 us
  Pallas kernels  62.6 us (94%)
  local copies, waits for them, and re-layouts  3.84 us (6%)
    pallas_call x1, Pallas kernels, fused_local(): pl.pallas_call(fused, out_shape=jax.ShapeDtypeStruct((seqs, block_rows, r...  62.6 us
    unnamed x9, local copies, waits for them, and re-layouts  3.84 us

profile of v3, /device:TPU:0, one launch (start us, length us, event | category | flops | bytes accessed | tf_op | source)
XLA Modules:
  0.0 66.5 jit_solution(8972835606976332734)
XLA Ops:
  0.0 0.0 copy-start
  0.0 1.0 %copy-done = bf16[3584,64]{0,1:T(8,128)(2,1)S(1)} copy-done((bf16[3584,64]{0,1:T(8,128)(2,1)S(1)}, bf16[3584,64]{0,1:T(8,128)(2,1)}, u32[]{:S(2)}) %copy-start) | copy-done | bytes 458776
  1.0 0.0 copy-start.1
  1.0 0.9 %copy-done.1 = bf16[1024,64]{0,1:T(8,128)(2,1)S(1)} copy-done((bf16[1024,64]{0,1:T(8,128)(2,1)S(1)}, bf16[1024,64]{0,1:T(8,128)(2,1)}, u32[]{:S(2)}) %copy-start.1) | copy-done | bytes 131096
  1.9 0.0 copy-start.2
  1.9 0.7 copy-done.2
  2.6 0.0 copy-start.3
  2.6 0.7 copy-done.3
  3.2 62.6 %shard_map.64 = f32[4,8,64]{2,1,0:T(8,128)S(1)} custom-call(bf16[3584,8192]{1,0:T(8,128)(2,1)} %acts.1, bf16[1024,8192]{1,0:T(8,128)(2,1)} %grads.1, bf16[64,3584]{1,0:T(8,128)(2,1)S(1)} %bitcast.3, bf16[64,1024]{1,0:T(8,128)(2,1)S(1)} %bitcast.4, s32[8]{0:T(128)S(1)} %copy-done.2, s32[4]{0:T(128)S(1)} %copy-done.3), custom_call_target="tpu_custom_call" | custom-call | flops 4831838208 | bytes 75497472 | tf_op jit(solution)/shard_map/pallas_call | solution.py:299
  65.8 0.6 copy.8
Async XLA Ops:
  0.0 1.0 %copy-start = (bf16[3584,64]{0,1:T(8,128)(2,1)S(1)}, bf16[3584,64]{0,1:T(8,128)(2,1)}, u32[]{:S(2)}) copy-start(bf16[3584,64]{0,1:T(8,128)(2,1)} %param.8) | copy-start | bytes 1376260
  1.0 0.9 %copy-start.1 = (bf16[1024,64]{0,1:T(8,128)(2,1)S(1)}, bf16[1024,64]{0,1:T(8,128)(2,1)}, u32[]{:S(2)}) copy-start(bf16[1024,64]{0,1:T(8,128)(2,1)} %param.9) | copy-start | bytes 393220
  1.9 0.7 copy-start.2
  2.6 0.7 copy-start.3
